TPU v7x, 32 devices: a whole 2x2x4 slice. The times are simulated.
32 devices in a mesh: rows: 8 (over z, x), rep: 4 (over y, core).
Axes of the slice: x: 2, y: 2, z: 4, core: 2. Of those that a mesh axis runs over, the one named last changes fastest.
Arguments:
- features: bfloat16 [4096, 256], P(('rows', 'rep')), may hold values from -6 to 6
- weight: bfloat16 [256, 256], replicated, may hold values from -0.375 to 0.375
- bias_terms: float32 [256], replicated, may hold values from -3 to 3
- tile_data: bfloat16 [8, 4, 8, 128, 128], P('rows'), may hold values from -0.1875 to 0.1875
- tile_row: int32 [8, 4, 8], P('rows'), may hold values from 0 to 3
- tile_col: int32 [8, 4, 8], P('rows'), may hold values from 0 to 7
- tile_count: int32 [8, 4], P('rows'), may hold values from 1 to 8, as said below
- grad_out: bfloat16 [4096, 256], P(('rows', 'rep')), may hold values from -6 to 6
Outputs:
- layer_out: bfloat16 [4096, 256], P(('rows', 'rep'))
- weight_grad: float32 [256, 256], replicated
- bias_grad: float32 [256], replicated
Inputs may be any that keep to these rules, and one draw needn't show every extreme that they name: `tile_count`: some group's stripe has all 8 slots live in every draw.
All inputs are finite; a program needn't handle non-finite values.
Results may differ from a plain program's by a relative error of at most 0.015.
Values may be sent and summed in bfloat16 or wider, within the bound.
A program may use at most 64 MiB of HBM per device.

v0:
```python
import jax
import jax.numpy as jnp
from jax import lax
from jax.sharding import PartitionSpec as P


def slots_wide(tile_set, row_set, col_set, live_set, blocks, row_count):
    picked = jnp.take(blocks, col_set, axis=0)
    product = jnp.einsum("tij,tjf->tif", tile_set, picked, preferred_element_type=jnp.float32)
    local_ids = jnp.arange(row_count, dtype=jnp.int32)
    select = ((row_set[None, :] == local_ids[:, None]) & live_set[None, :]).astype(jnp.float32)
    return jnp.einsum("bt,tif->bif", select, product)


def propagate(tile_set, row_set, col_set, count_set, blocks, row_count, slot_fn):
    stripes, capacity = row_set.shape
    block_size = tile_set.shape[-1]
    slot_ids = jnp.arange(capacity, dtype=jnp.int32)
    live_set = slot_ids[None, :] < count_set[:, None]
    accumulated = slot_fn(
        tile_set.reshape(-1, block_size, block_size),
        row_set.reshape(-1),
        col_set.reshape(-1),
        live_set.reshape(-1),
        blocks,
        row_count,
    )
    return accumulated


def shards(features, weight, bias_terms, tile_data, tile_row, tile_col, tile_count, grad_out):
    block_size = tile_data.shape[-1]
    feature_width = features.shape[1]
    row_count = lax.axis_size("rep")
    rep_index = lax.axis_index("rep")
    own_tiles = lax.dynamic_slice_in_dim(tile_data[0], rep_index, 1, 0)
    own_rows = lax.dynamic_slice_in_dim(tile_row[0], rep_index, 1, 0)
    own_cols = lax.dynamic_slice_in_dim(tile_col[0], rep_index, 1, 0)
    own_count = lax.dynamic_slice_in_dim(tile_count[0], rep_index, 1, 0)
    stripe_nodes = lax.all_gather(features, "rows", axis=0, tiled=True)
    blocks = stripe_nodes.reshape(-1, block_size, feature_width)
    partial_value = propagate(
        own_tiles, own_rows, own_cols, own_count, blocks, row_count, slots_wide
    )
    partial_value = partial_value.reshape(row_count * block_size, feature_width)
    propagated = lax.psum_scatter(partial_value, "rep", scatter_dimension=0, tiled=True).astype(
        jnp.bfloat16
    )
    preact = jnp.dot(propagated, weight, preferred_element_type=jnp.float32) + bias_terms
    sigma = jax.nn.sigmoid(preact)
    layer_out = (preact * sigma).astype(jnp.bfloat16)
    slope = sigma * (1.0 + preact * (1.0 - sigma))
    grad_pre = (grad_out.astype(jnp.float32) * slope).astype(jnp.bfloat16)
    weight_term = lax.dot_general(
        propagated, grad_pre, (((0,), (0,)), ((), ())), preferred_element_type=jnp.float32
    )
    bias_term = jnp.sum(grad_pre.astype(jnp.float32), axis=0)
    weight_grad, bias_grad = lax.psum((weight_term, bias_term), ("rows", "rep"))
    return (layer_out, weight_grad, bias_grad)


def solution(mesh):
    placed = (
        P(("rows", "rep"), None),
        P(),
        P(),
        P("rows", None, None, None, None),
        P("rows", None, None),
        P("rows", None, None),
        P("rows", None),
        P(("rows", "rep"), None),
    )
    return jax.shard_map(
        shards,
        mesh=mesh,
        in_specs=placed,
        out_specs=(P(("rows", "rep"), None), P(), P()),
        check_vma=False,
    )
```

profile of v0, /device:TPU:0, one launch (start us, length us, event | category | flops | bytes accessed | tf_op | source)
XLA Modules:
  0.0 209.0 jit_solution(16761925454625325596)
XLA Ops:
  7.2 0.0 copy-start
  7.2 0.0 reduce-scatter.2.cloned.1.call-start
  7.2 0.0 copy-start.4
  7.2 0.8 copy-done.4
  8.0 0.0 copy-start.6
  8.0 33.2 %all_gather.3 = bf16[1024,256]{1,0:T(8,128)(2,1)S(1)} all-gather(bf16[128,256]{1,0:T(8,128)(2,1)} %param.8), channel_id=1, replica_groups=mesh['rows'=8,'rep'=4] {'rows'}, dimensions={0}, use_global_device_ids=true | all-gather | bytes 589824 | tf_op jit(solution)/shard_map/all_gather | solution.py:40
  41.3 0.0 copy-done.6
  41.3 0.6 constant_dynamic-slice_fusion.1
  41.9 0.6 iota_compare_fusion.1
  42.5 0.7 fusion.17
  43.2 0.6 gather_fusion
  43.8 0.0 copy-done
  43.8 0.4 fusion.2
  44.2 0.4 fusion
  44.6 0.9 copy.11
  45.5 0.0 copy-start.2
  45.5 0.0 copy-start.3
  45.5 0.0 copy-start.5
  45.5 0.0 reduce-scatter.2.cloned.1.call-update
  45.5 0.0 all-reduce.2.cloned.1.call-start
  45.5 22.9 %reduce-scatter.2.cloned.1.call-done = f32[128,256]{1,0:T(8,128)} async-done(((f32[512,256]{1,0:T(8,128)}), f32[128,256]{1,0:T(8,128)}) %reduce-scatter.2.cloned.1.call-update) | async-done | bytes 131088 | tf_op jit(solution)/shard_map/reduce_scatter | solution.py:46
  68.4 0.0 copy-done.2
  68.4 0.0 copy-done.3
  68.4 0.0 copy-done.5
  68.4 0.0 copy-start.1
  68.4 1.8 convert_reduce_fusion
  70.3 0.0 copy-done.1
  70.3 0.9 fusion.8
  71.2 0.0 all-reduce.2.cloned.1.call-update
  71.2 39.4 %psum.15 = f32[256]{0:T(256)} all-reduce(f32[256]{0:T(256)S(1)} %get-tuple-element.3), channel_id=1, replica_groups=mesh['rows'=8,'rep'=4] {'rows','rep'}, use_global_device_ids=true, to_apply=%region_3.4 | all-reduce | flops 256 | bytes 2048 | tf_op jit(solution)/shard_map/psum | solution.py:58
  110.6 89.9 %all-reduce.2.cloned.1.call-done = f32[256,256]{1,0:T(8,128)} async-done(((f32[256,256]{1,0:T(8,128)}), f32[256,256]{1,0:T(8,128)}) %all-reduce.2.cloned.1.call-update) | async-done | bytes 262160 | tf_op jit(solution)/shard_map/psum | solution.py:58
  200.5 1.7 copy.16
  (3 shorter events, 0.0 us)
Async XLA Ops:
  7.2 36.6 %copy-start = (bf16[1,4,8,128,128]{4,3,2,1,0:T(8,128)(2,1)S(1)}, bf16[1,4,8,128,128]{4,3,2,1,0:T(8,128)(2,1)}, u32[]{:S(2)}) copy-start(bf16[1,4,8,128,128]{4,3,2,1,0:T(8,128)(2,1)} %param.11) | copy-start | bytes 3145732
  7.2 61.2 %reduce-scatter.2.cloned.1.call-start = ((), (), s32[]{:S(2)}) async-start(), calls=%async_computation.1 | async-start | bytes 655360 | tf_op jit(solution)/shard_map/reduce_scatter | solution.py:46
  7.2 0.8 copy-start.4
  8.0 33.2 %copy-start.6 = (s32[1,4]{1,0:T(1,128)S(1)}, s32[1,4]{1,0:T(1,128)}, u32[]{:S(2)}) copy-start(s32[1,4]{1,0:T(1,128)} %param.14) | copy-start | bytes 52
  45.5 23.0 %copy-start.2 = (bf16[256,256]{1,0:T(8,128)(2,1)S(1)}, bf16[256,256]{1,0:T(8,128)(2,1)}, u32[]{:S(2)}) copy-start(bf16[256,256]{1,0:T(8,128)(2,1)} %param.9) | copy-start | bytes 393220
  45.5 23.0 %copy-start.3 = (bf16[128,256]{1,0:T(8,128)(2,1)S(1)}, bf16[128,256]{1,0:T(8,128)(2,1)}, u32[]{:S(2)}) copy-start(bf16[128,256]{1,0:T(8,128)(2,1)} %param.15) | copy-start | bytes 196612
  45.5 23.0 %copy-start.5 = (f32[256]{0:T(256)S(1)}, f32[256]{0:T(256)}, u32[]{:S(2)}) copy-start(f32[256]{0:T(256)} %param.10) | copy-start | bytes 3076
  45.5 155.0 %all-reduce.2.cloned.1.call-start = ((), (), s32[]{:S(2)}) async-start(), calls=%async_computation.2 | async-start | bytes 524288 | tf_op jit(solution)/shard_map/psum | solution.py:58
  68.4 1.8 copy-start.1
Sparse Core Ops, SparseCore 0:
  45.6 22.7 reduce-scatter.1
  75.4 125.0 all-reduce.1
where the time goes:
time: 209 us
  waiting for transfers between devices  113 us (54%)
  blocking collectives  72.6 us (35%)
  between operations  14.1 us (7%)
  local copies, waits for them, and re-layouts  5.19 us (2%)
  matrix products  3.51 us (2%)
    psum x1, waiting for transfers between devices, shards(): weight_grad, bias_grad = lax.psum((weight_term, bias_term), ('rows', 'rep'))  89.9 us
    psum x1, blocking collectives, shards(): weight_grad, bias_grad = lax.psum((weight_term, bias_term), ('rows', 'rep'))  39.4 us
    all_gather x1, blocking collectives, shards(): stripe_nodes = lax.all_gather(features, 'rows', axis=0, tiled=True)  33.2 us
    reduce_scatter x1, waiting for transfers between devices, shards(): lax.psum_scatter(partial_value, 'rep', scatter_dimension=0, tiled=True)  22.9 us
  transfers between devices with their start and end apart: 2, of which 2 were waited for; matrix products, arithmetic and copies ran while one was open for 0% of the time, Pallas kernels for 0%

commit v1 on v0

v1 whole, which is shorter than its diff:
```python
import functools

import jax
import jax.numpy as jnp
from jax import lax
from jax.experimental import pallas as pl
from jax.experimental.pallas import tpu as pltpu
from jax.sharding import PartitionSpec as P

MESH = pl.DeviceIdType.MESH


def xor(value, mask):
    bit = 1
    while bit <= mask:
        if mask & bit:
            value = value + bit - 2 * bit * ((value // bit) % 2)
        bit *= 2
    return value


def kernel(
    n_rows, n_rep, staged,
    feat_hbm, weight_hbm, bias_hbm, tile_hbm, row_ref, col_ref, count_ref, gout_hbm,
    out_ref, wgrad_ref, bgrad_ref,
    feat, tiles, weight, bias, gout, part, part_in, term, term_in, slab, piece, piece_in,
    local_sem, g_send, g_recv, x_send, x_recv, w1_send, w1_recv,
    w2_send, w2_recv, w3_send, w3_recv, w4_send, w4_recv,
):
    me = lax.axis_index("rows")
    rep = lax.axis_index("rep")
    capacity, block = tiles.shape[0], tiles.shape[1]
    width = weight.shape[1]
    own_rows = width // n_rep

    loads = [
        pltpu.make_async_copy(feat_hbm, feat.at[me], local_sem.at[0]),
        pltpu.make_async_copy(tile_hbm.at[0, rep], tiles, local_sem.at[1]),
        pltpu.make_async_copy(weight_hbm, weight, local_sem.at[2]),
        pltpu.make_async_copy(bias_hbm, bias, local_sem.at[3]),
        pltpu.make_async_copy(gout_hbm, gout, local_sem.at[4]),
    ]
    for load in loads:
        load.start()

    def to_rows(mask, src, dst, send, recv):
        return pltpu.make_async_remote_copy(
            src_ref=src, dst_ref=dst, send_sem=send, recv_sem=recv,
            device_id=(xor(me, mask), rep), device_id_type=MESH)

    def to_rep(mask, src, dst, send, recv):
        return pltpu.make_async_remote_copy(
            src_ref=src, dst_ref=dst, send_sem=send, recv_sem=recv,
            device_id=(me, xor(rep, mask)), device_id_type=MESH)

    barrier = pltpu.get_barrier_semaphore()
    for mask in range(1, n_rows):
        pl.semaphore_signal(barrier, inc=1, device_id=(xor(me, mask), rep), device_id_type=MESH)
    for mask in range(1, n_rep):
        pl.semaphore_signal(barrier, inc=1, device_id=(me, xor(rep, mask)), device_id_type=MESH)
    pl.semaphore_wait(barrier, n_rows + n_rep - 2)

    def gather(mask, block_mask, sem):
        where = feat.at[xor(me, block_mask)]
        source = feat_hbm if block_mask == 0 else where
        return to_rows(mask, source, where, g_send.at[sem], g_recv.at[sem])

    sends = [gather(1, 0, 1)]
    for mask in range(2, n_rows, 2):
        sends.append(gather(mask, 0, mask))
    for send in sends:
        send.start()

    def arrived(mask):
        where = feat.at[xor(me, mask)]
        to_rows(1, where, where, g_send.at[mask], g_recv.at[mask]).wait_recv()

    for mask in range(2, n_rows, 2):
        arrived(mask)
        send = gather(1, mask, mask + 1)
        send.start()
        sends.append(send)
    for mask in range(1, n_rows, 2):
        arrived(mask)
    loads[0].wait()
    loads[1].wait()

    rows_of = [row_ref[0, rep, slot] for slot in range(capacity)]
    live = [slot < count_ref[0, rep] for slot in range(capacity)]
    picked = jnp.concatenate([feat[col_ref[0, rep, slot]] for slot in range(capacity)], axis=0)
    none = jnp.zeros((block, block), jnp.bfloat16)

    def wide(target):
        return jnp.concatenate(
            [jnp.where((rows_of[slot] == target) & live[slot], tiles[slot], none)
             for slot in range(capacity)], axis=1)

    stacked = jnp.concatenate([wide(xor(rep, mask)) for mask in range(n_rep)], axis=0)
    partial = jnp.dot(stacked, picked, preferred_element_type=jnp.float32)
    part[...] = partial[block:].reshape(n_rep - 1, block, width).astype(jnp.bfloat16)
    exchange = [
        to_rep(mask, part.at[mask - 1], part_in.at[mask - 1], x_send.at[mask - 1], x_recv.at[mask - 1])
        for mask in range(1, n_rep)
    ]
    for copy in reversed(exchange):
        copy.start()
    for load in loads[2:]:
        load.wait()
    total = partial[:block]
    for mask in range(1, n_rep):
        exchange[mask - 1].wait_recv()
        total = total + part_in[mask - 1].astype(jnp.float32)

    propagated = total.astype(jnp.bfloat16)
    preact = jnp.dot(propagated, weight[...], preferred_element_type=jnp.float32) + bias[...]
    sigma = jax.nn.sigmoid(preact)
    slope = sigma * (1.0 + preact * (1.0 - sigma))
    grad_pre = (gout[...].astype(jnp.float32) * slope).astype(jnp.bfloat16)
    weight_term = lax.dot_general(
        propagated, grad_pre, (((0,), (0,)), ((), ())), preferred_element_type=jnp.float32)
    bias_term = jnp.sum(grad_pre.astype(jnp.float32).reshape(block // 8, 8, width), axis=0)
    for place in range(n_rep):
        term[place, :own_rows] = weight_term[place * own_rows:(place + 1) * own_rows]
        term[place, own_rows:] = bias_term

    scatter = [
        to_rep(mask, term.at[xor(rep, mask)], term_in.at[mask - 1], w1_send.at[mask - 1], w1_recv.at[mask - 1])
        for mask in range(1, n_rep)
    ]
    for copy in reversed(scatter):
        copy.start()
    out_ref[...] = (preact * sigma).astype(jnp.bfloat16)
    mine = term[rep]
    for mask in range(1, n_rep):
        scatter[mask - 1].wait_recv()
        mine = mine + term_in[mask - 1]

    base = pl.multiple_of(rep * own_rows, own_rows)
    pending = []
    if staged:
        share = own_rows // n_rows
        for place in range(n_rows):
            piece[place, :share] = mine[place * share:(place + 1) * share]
            piece[place, share:] = mine[own_rows:]
        spread = [
            to_rows(mask, piece.at[xor(me, mask)], piece_in.at[mask - 1],
                    w2_send.at[mask - 1], w2_recv.at[mask - 1])
            for mask in range(1, n_rows)
        ]
        for copy in spread:
            copy.start()
        done = piece[me]
        for mask in range(1, n_rows):
            spread[mask - 1].wait_recv()
            done = done + piece_in[mask - 1]
        final_bias = done[share:]

        def share_of(index):
            return wgrad_ref.at[pl.ds(pl.multiple_of(base + index * share, share), share)]

        wgrad_ref[pl.ds(pl.multiple_of(base + me * share, share), share)] = done[:share]
        back = [
            to_rows(mask, share_of(me), share_of(me), w3_send.at[mask - 1], w3_recv.at[mask - 1])
            for mask in range(1, n_rows)
        ]
        for copy in back:
            copy.start()
        for mask in range(1, n_rows):
            where = share_of(xor(me, mask))
            to_rows(mask, where, where, w3_send.at[mask - 1], w3_recv.at[mask - 1]).wait_recv()
        pending = spread + back
    else:
        step = 0
        while (1 << step) < n_rows:
            slab[step] = mine
            copy = to_rows(1 << step, slab.at[step], piece_in.at[step], w2_send.at[step], w2_recv.at[step])
            copy.start()
            copy.wait_recv()
            mine = mine + piece_in[step]
            pending.append(copy)
            step += 1
        final_bias = mine[own_rows:]
        wgrad_ref[pl.ds(base, own_rows)] = mine[:own_rows]

    def slab_of(index):
        return wgrad_ref.at[pl.ds(pl.multiple_of(index * own_rows, own_rows), own_rows)]

    final = [
        to_rep(mask, slab_of(rep), slab_of(rep), w4_send.at[mask - 1], w4_recv.at[mask - 1])
        for mask in range(1, n_rep)
    ]
    for copy in reversed(final):
        copy.start()
    bgrad_ref[...] = jnp.sum(final_bias, axis=0, keepdims=True)
    for copy in sends + exchange + scatter + pending + final:
        copy.wait_send()
    for mask in range(1, n_rep):
        where = slab_of(xor(rep, mask))
        to_rep(mask, where, where, w4_send.at[mask - 1], w4_recv.at[mask - 1]).wait_recv()


def shards(features, weight, bias_terms, tile_data, tile_row, tile_col, tile_count, grad_out):
    n_rows, n_rep = lax.axis_size("rows"), lax.axis_size("rep")
    block, width = features.shape
    capacity = tile_data.shape[2]
    own_rows = width // n_rep
    staged = own_rows % (8 * n_rows) == 0
    share = own_rows // n_rows if staged else 8
    steps = 1 if staged else (n_rows - 1).bit_length()
    whole = (own_rows + 8, width)
    vmem = pl.BlockSpec(memory_space=pltpu.VMEM)
    smem = pl.BlockSpec(memory_space=pltpu.SMEM)
    hbm = pl.BlockSpec(memory_space=pl.ANY)
    dma = pltpu.SemaphoreType.DMA
    layer_out, weight_grad, bias_grad = pl.pallas_call(
        functools.partial(kernel, n_rows, n_rep, staged),
        out_shape=(
            jax.ShapeDtypeStruct((block, width), jnp.bfloat16),
            jax.ShapeDtypeStruct((width, width), jnp.float32),
            jax.ShapeDtypeStruct((1, width), jnp.float32),
        ),
        in_specs=[hbm, hbm, hbm, hbm, smem, smem, smem, hbm],
        out_specs=(vmem, vmem, vmem),
        scratch_shapes=[
            pltpu.VMEM((n_rows, block, width), jnp.bfloat16),
            pltpu.VMEM((capacity, block, block), jnp.bfloat16),
            pltpu.VMEM((width, width), jnp.bfloat16),
            pltpu.VMEM((1, width), jnp.float32),
            pltpu.VMEM((block, width), jnp.bfloat16),
            pltpu.VMEM((n_rep - 1, block, width), jnp.bfloat16),
            pltpu.VMEM((n_rep - 1, block, width), jnp.bfloat16),
            pltpu.VMEM((n_rep,) + whole, jnp.float32),
            pltpu.VMEM((n_rep - 1,) + whole, jnp.float32),
            pltpu.VMEM((steps,) + whole, jnp.float32),
            pltpu.VMEM((n_rows, share + 8, width), jnp.float32),
            pltpu.VMEM((n_rows - 1, share + 8, width) if staged else (steps,) + whole, jnp.float32),
            dma((5,)),
            dma((n_rows,)), dma((n_rows,)),
            dma((n_rep - 1,)), dma((n_rep - 1,)),
            dma((n_rep - 1,)), dma((n_rep - 1,)),
            dma((n_rows - 1,)), dma((n_rows - 1,)),
            dma((n_rows - 1,)), dma((n_rows - 1,)),
            dma((n_rep - 1,)), dma((n_rep - 1,)),
        ],
        compiler_params=pltpu.CompilerParams(
            collective_id=0, has_side_effects=True, vmem_limit_bytes=40 * 1024 * 1024),
    )(features, weight, bias_terms.reshape(1, width), tile_data, tile_row, tile_col, tile_count, grad_out)
    return layer_out, weight_grad, bias_grad.reshape(width)


def solution(mesh):
    placed = (
        P(("rows", "rep"), None),
        P(),
        P(),
        P("rows", None, None, None, None),
        P("rows", None, None),
        P("rows", None, None),
        P("rows", None),
        P(("rows", "rep"), None),
    )
    return jax.shard_map(
        shards,
        mesh=mesh,
        in_specs=placed,
        out_specs=(P(("rows", "rep"), None), P(), P()),
        check_vma=False,
    )
```

time: 209 us -> 48.5 us (0.23)
  waiting for transfers between devices: 113 us -> 0 us
  blocking collectives: 72.6 us -> 0 us
  Pallas kernels: 0 us -> 39.8 us
  between operations: 14.1 us -> 0.67 us
  matrix products: 3.51 us -> 0 us
  local copies, waits for them, and re-layouts: 5.19 us -> 7.74 us
    psum x1 -> x0, waiting for transfers between devices: 89.9 us -> none  [shards(): weight_grad, bias_grad = lax.psum((weight_term, bias_term), ('rows', 'rep'))]
    pallas_call x0 -> x1, Pallas kernels: none -> 39.8 us  [shards(): pl.pallas_call(functools.partial(kernel, n_rows, n_rep, staged), out_shap...]
    psum x1 -> x0, blocking collectives: 39.4 us -> none  [shards(): weight_grad, bias_grad = lax.psum((weight_term, bias_term), ('rows', 'rep'))]
    all_gather x1 -> x0, blocking collectives: 33.2 us -> none  [shards(): stripe_nodes = lax.all_gather(features, 'rows', axis=0, tiled=True)]
    reduce_scatter x1 -> x0, waiting for transfers between devices: 22.9 us -> none  [shards(): lax.psum_scatter(partial_value, 'rep', scatter_dimension=0, tiled=True)]
    unnamed x15 -> x19, local copies, waits for them, and re-layouts: 2.45 us -> 7.74 us
    dot_general x4 -> x0, matrix products: 3.51 us -> none  [the longest x1 1.83 us: shards(): jnp.dot(propagated, weight, preferred_element_type=jnp.float32) + bias_terms]
  transfers between devices with their start and end apart: 2 -> 0, of which waited for: 2 -> 0; matrix products, arithmetic and copies ran while one was open for 0% -> 0% of each run, Pallas kernels for 0% -> 0%
where the time goes in v1:
time: 48.5 us; the launch traced here: 48.2 us
  Pallas kernels  39.8 us (82%)
  local copies, waits for them, and re-layouts  7.74 us (16%)
  between operations  0.67 us (1%)
    pallas_call x1, Pallas kernels, shards(): pl.pallas_call(functools.partial(kernel, n_rows, n_rep, staged), out_shap...  39.8 us
    unnamed x19, local copies, waits for them, and re-layouts  7.74 us

profile of v1, /device:TPU:0, one launch (start us, length us, event | category | flops | bytes accessed | tf_op | source)
XLA Modules:
  0.0 48.2 jit_solution(12131224172293834048)
XLA Ops:
  0.6 0.0 copy-start.7
  0.6 0.0 copy-start.6
  0.7 0.6 %copy-done.7 = s32[1,4]{1,0:T(1,128)S(1)} copy-done((s32[1,4]{1,0:T(1,128)S(1)}, s32[1,4]{1,0:T(1,128)}, u32[]{:S(2)}) %copy-start.7) | copy-done | bytes 40
  1.3 0.0 copy-done.6
  1.3 0.0 copy-start
  1.3 1.2 %copy-done = bf16[1,4,8,128,128]{4,3,2,1,0:T(8,128)(2,1)S(1)} copy-done((bf16[1,4,8,128,128]{4,3,2,1,0:T(8,128)(2,1)S(1)}, bf16[1,4,8,128,128]{4,3,2,1,0:T(8,128)(2,1)}, u32[]{:S(2)}) %copy-start) | copy-done | bytes 1048600
  2.6 0.0 copy-start.1
  2.6 0.9 %copy-done.1 = bf16[256,256]{1,0:T(8,128)(2,1)S(1)} copy-done((bf16[256,256]{1,0:T(8,128)(2,1)S(1)}, bf16[256,256]{1,0:T(8,128)(2,1)}, u32[]{:S(2)}) %copy-start.1) | copy-done | bytes 131096
  3.5 0.0 copy-start.2
  3.5 0.8 %copy-done.2 = bf16[128,256]{1,0:T(8,128)(2,1)S(1)} copy-done((bf16[128,256]{1,0:T(8,128)(2,1)S(1)}, bf16[128,256]{1,0:T(8,128)(2,1)}, u32[]{:S(2)}) %copy-start.2) | copy-done | bytes 65560
  4.3 0.0 copy-start.3
  4.3 0.8 %copy-done.3 = bf16[128,256]{1,0:T(8,128)(2,1)S(1)} copy-done((bf16[128,256]{1,0:T(8,128)(2,1)S(1)}, bf16[128,256]{1,0:T(8,128)(2,1)}, u32[]{:S(2)}) %copy-start.3) | copy-done | bytes 65560
  5.1 0.0 copy-start.4
  5.1 0.7 %copy-done.4 = s32[1,4,8]{2,1,0:T(4,128)S(1)} copy-done((s32[1,4,8]{2,1,0:T(4,128)S(1)}, s32[1,4,8]{2,1,0:T(4,128)}, u32[]{:S(2)}) %copy-start.4) | copy-done | bytes 152
  5.8 0.0 copy-start.5
  5.8 0.7 %copy-done.5 = s32[1,4,8]{2,1,0:T(4,128)S(1)} copy-done((s32[1,4,8]{2,1,0:T(4,128)S(1)}, s32[1,4,8]{2,1,0:T(4,128)}, u32[]{:S(2)}) %copy-start.5) | copy-done | bytes 152
  6.5 39.8 %shard_map.103 = (bf16[128,256]{1,0:T(8,128)(2,1)S(1)}, f32[256,256]{1,0:T(8,128)S(1)}, f32[1,256]{1,0:T(1,128)S(1)}) custom-call(bf16[128,256]{1,0:T(8,128)(2,1)S(1)} %copy-done.2, bf16[256,256]{1,0:T(8,128)(2,1)S(1)} %copy-done.1, f32[1,256]{1,0:T(1,128)S(1)} %bitcast.3, bf16[1,4,8,128,128]{4,3,2,1,0:T(8,128)(2,1)S(1)} %copy-done, ...), custom_call_target="tpu_custom_call" | custom-call | tf_op jit(solution)/shard_map/pallas_call | solution.py:215
  46.3 0.6 %copy.14 = bf16[128,256]{1,0:T(8,128)(2,1)} copy(bf16[128,256]{1,0:T(8,128)(2,1)S(1)} %get-tuple-element.12) | data formatting | bytes 131072
  46.9 0.7 %copy.15 = f32[256,256]{1,0:T(8,128)} copy(f32[256,256]{1,0:T(8,128)S(1)} %get-tuple-element.13) | data formatting | bytes 524288
  47.6 0.6 %copy.16 = f32[256]{0:T(256)} copy(f32[256]{0:T(256)S(1)} %bitcast.2) | data formatting | bytes 2048
Async XLA Ops:
  0.6 0.7 %copy-start.7 = (s32[1,4]{1,0:T(1,128)S(1)}, s32[1,4]{1,0:T(1,128)}, u32[]{:S(2)}) copy-start(s32[1,4]{1,0:T(1,128)} %count_ref.1) | copy-start | bytes 52
  0.6 0.7 %copy-start.6 = (f32[256]{0:T(256)S(1)}, f32[256]{0:T(256)}, u32[]{:S(2)}) copy-start(f32[256]{0:T(256)} %param.10) | copy-start | bytes 3076
  1.3 1.2 %copy-start = (bf16[1,4,8,128,128]{4,3,2,1,0:T(8,128)(2,1)S(1)}, bf16[1,4,8,128,128]{4,3,2,1,0:T(8,128)(2,1)}, u32[]{:S(2)}) copy-start(bf16[1,4,8,128,128]{4,3,2,1,0:T(8,128)(2,1)} %tile_hbm.1) | copy-start | bytes 3145732
  2.6 0.9 %copy-start.1 = (bf16[256,256]{1,0:T(8,128)(2,1)S(1)}, bf16[256,256]{1,0:T(8,128)(2,1)}, u32[]{:S(2)}) copy-start(bf16[256,256]{1,0:T(8,128)(2,1)} %weight_hbm.1) | copy-start | bytes 393220
  3.5 0.8 %copy-start.2 = (bf16[128,256]{1,0:T(8,128)(2,1)S(1)}, bf16[128,256]{1,0:T(8,128)(2,1)}, u32[]{:S(2)}) copy-start(bf16[128,256]{1,0:T(8,128)(2,1)} %feat_hbm.1) | copy-start | bytes 196612
  4.3 0.8 %copy-start.3 = (bf16[128,256]{1,0:T(8,128)(2,1)S(1)}, bf16[128,256]{1,0:T(8,128)(2,1)}, u32[]{:S(2)}) copy-start(bf16[128,256]{1,0:T(8,128)(2,1)} %gout_hbm.1) | copy-start | bytes 196612
  5.1 0.7 %copy-start.4 = (s32[1,4,8]{2,1,0:T(4,128)S(1)}, s32[1,4,8]{2,1,0:T(4,128)}, u32[]{:S(2)}) copy-start(s32[1,4,8]{2,1,0:T(4,128)} %row_ref.1) | copy-start | bytes 388
  5.8 0.7 %copy-start.5 = (s32[1,4,8]{2,1,0:T(4,128)S(1)}, s32[1,4,8]{2,1,0:T(4,128)}, u32[]{:S(2)}) copy-start(s32[1,4,8]{2,1,0:T(4,128)} %col_ref.1) | copy-start | bytes 388

commit v2 on v1

v2 whole, which is shorter than its diff:
```python
import functools

import jax
import jax.numpy as jnp
from jax import lax
from jax.experimental import pallas as pl
from jax.experimental.pallas import tpu as pltpu
from jax.sharding import PartitionSpec as P

MESH = pl.DeviceIdType.MESH
SHARE_TYPE = jnp.bfloat16


def xor(value, mask):
    bit = 1
    while bit <= mask:
        if mask & bit:
            value = value + bit - 2 * bit * ((value // bit) % 2)
        bit *= 2
    return value


def kernel(
    n_rows, n_rep, direct,
    feat_hbm, weight_hbm, bias_hbm, tile_hbm, row_hbm, col_hbm, count_hbm, gout_hbm,
    out_ref, wgrad_ref, bgrad_ref,
    feat, tiles, weight, bias, gout, part, part_in, term, term_in, ring, ring_in, bias_out, bias_in, piece, piece_in, share_in,
    row_ref, col_ref, count_ref, local_sem, g_send, g_recv, x_send, x_recv, w1_send, w1_recv,
    w2_send, w2_recv, w4_send, w4_recv, d_sem, b_sem,
):
    me = lax.axis_index("rows")
    rep = lax.axis_index("rep")
    capacity, block = tiles.shape[0], tiles.shape[1]
    width = weight.shape[1]
    own_rows = width // n_rep

    def to_rows(mask, src, dst, send, recv):
        return pltpu.make_async_remote_copy(
            src_ref=src, dst_ref=dst, send_sem=send, recv_sem=recv,
            device_id=(xor(me, mask), rep), device_id_type=MESH)

    def to_rep(mask, src, dst, send, recv):
        return pltpu.make_async_remote_copy(
            src_ref=src, dst_ref=dst, send_sem=send, recv_sem=recv,
            device_id=(me, xor(rep, mask)), device_id_type=MESH)

    barrier = pltpu.get_barrier_semaphore()
    for mask in range(1, n_rows):
        pl.semaphore_signal(barrier, inc=1, device_id=(xor(me, mask), rep), device_id_type=MESH)
    for mask in range(1, n_rep):
        pl.semaphore_signal(barrier, inc=1, device_id=(me, xor(rep, mask)), device_id_type=MESH)
    loads = [
        pltpu.make_async_copy(feat_hbm, feat.at[me], local_sem.at[0]),
        pltpu.make_async_copy(tile_hbm.at[0, rep], tiles, local_sem.at[1]),
        pltpu.make_async_copy(weight_hbm, weight, local_sem.at[2]),
        pltpu.make_async_copy(bias_hbm, bias, local_sem.at[3]),
        pltpu.make_async_copy(gout_hbm, gout, local_sem.at[4]),
        pltpu.make_async_copy(row_hbm, row_ref, local_sem.at[5]),
        pltpu.make_async_copy(col_hbm, col_ref, local_sem.at[6]),
        pltpu.make_async_copy(count_hbm, count_ref, local_sem.at[7]),
    ]
    for load in loads:
        load.start()
    pl.semaphore_wait(barrier, n_rows + n_rep - 2)

    def gather(mask, block_mask, sem):
        where = feat.at[xor(me, block_mask)]
        source = feat_hbm if block_mask == 0 else where
        return to_rows(mask, source, where, g_send.at[sem], g_recv.at[sem])

    sends = [gather(1, 0, 1)]
    for mask in range(2, n_rows, 2):
        sends.append(gather(mask, 0, mask))
    for send in sends:
        send.start()

    def arrived(mask):
        where = feat.at[xor(me, mask)]
        to_rows(1, where, where, g_send.at[mask], g_recv.at[mask]).wait_recv()

    for mask in range(2, n_rows, 2):
        arrived(mask)
        send = gather(1, mask, mask + 1)
        send.start()
        sends.append(send)
    for mask in range(1, n_rows, 2):
        arrived(mask)
    loads[0].wait()
    loads[1].wait()
    for load in loads[5:]:
        load.wait()

    rows_of = [row_ref[0, rep, slot] for slot in range(capacity)]
    live = [slot < count_ref[0, rep] for slot in range(capacity)]
    picked = jnp.concatenate([feat[col_ref[0, rep, slot]] for slot in range(capacity)], axis=0)
    none = jnp.zeros((block, block), jnp.bfloat16)

    def wide(target):
        return jnp.concatenate(
            [jnp.where((rows_of[slot] == target) & live[slot], tiles[slot], none)
             for slot in range(capacity)], axis=1)

    stacked = jnp.concatenate([wide(xor(rep, mask)) for mask in range(n_rep)], axis=0)
    partial = jnp.dot(stacked, picked, preferred_element_type=jnp.float32)
    part[...] = partial[block:].reshape(n_rep - 1, block, width).astype(jnp.bfloat16)
    exchange = [
        to_rep(mask, part.at[mask - 1], part_in.at[mask - 1], x_send.at[mask - 1], x_recv.at[mask - 1])
        for mask in range(1, n_rep)
    ]
    for copy in reversed(exchange):
        copy.start()
    for load in loads[2:5]:
        load.wait()
    total = partial[:block]
    for mask in range(1, n_rep):
        exchange[mask - 1].wait_recv()
        total = total + part_in[mask - 1].astype(jnp.float32)

    propagated = total.astype(jnp.bfloat16)
    preact = jnp.dot(propagated, weight[...], preferred_element_type=jnp.float32) + bias[...]
    sigma = jax.nn.sigmoid(preact)
    slope = sigma * (1.0 + preact * (1.0 - sigma))
    grad_pre = (gout[...].astype(jnp.float32) * slope).astype(jnp.bfloat16)
    weight_term = lax.dot_general(
        propagated, grad_pre, (((0,), (0,)), ((), ())), preferred_element_type=jnp.float32)
    bias_term = jnp.sum(grad_pre.astype(jnp.float32).reshape(block // 8, 8, width), axis=0)
    if direct:
        n_all = n_rows * n_rep
        here = me * n_rep + rep
        piece_rows, piece_cols = piece.shape[1:]
        across = width // piece_cols

        def place_of(index):
            top, left = index // across * piece_rows, index % across * piece_cols
            return slice(top, top + piece_rows), slice(left, left + piece_cols)

        def to_all(mask, src, dst, stage):
            peer = (xor(me, mask // n_rep), xor(rep, mask % n_rep))
            return pltpu.make_async_remote_copy(
                src_ref=src, dst_ref=dst, send_sem=d_sem.at[2 * stage], recv_sem=d_sem.at[2 * stage + 1],
                device_id=peer, device_id_type=MESH)

        order = sorted(range(1, n_all), key=lambda mask: -mask)
        for index in range(n_all):
            piece[index] = weight_term[place_of(index)].astype(jnp.bfloat16)
        for mask in order:
            to_all(mask, piece.at[xor(here, mask)], piece_in.at[mask - 1], 0).start()
        bias_out[0] = jnp.sum(bias_term, axis=0, keepdims=True)
        bias_rep = [
            to_rep(mask, bias_out.at[0], bias_in.at[mask - 1], b_sem.at[0, mask - 1], b_sem.at[1, mask - 1])
            for mask in range(1, n_rep)
        ]
        for copy in bias_rep:
            copy.start()
        out_ref[...] = (preact * sigma).astype(jnp.bfloat16)
        bias_sum = bias_out[0]
        for mask in range(1, n_rep):
            bias_rep[mask - 1].wait_recv()
            bias_sum = bias_sum + bias_in[mask - 1]
        bias_out[1] = bias_sum
        bias_rows = [
            to_rows(mask, bias_out.at[1], bias_in.at[n_rep - 2 + mask],
                    b_sem.at[0, n_rep - 2 + mask], b_sem.at[1, n_rep - 2 + mask])
            for mask in range(1, n_rows)
        ]
        done = piece[here].astype(jnp.float32)
        pltpu.make_async_copy(piece_in, piece_in, d_sem.at[1]).wait()
        for mask in range(1, n_all):
            done = done + piece_in[mask - 1].astype(jnp.float32)
        share_in[here] = done.astype(share_in.dtype)
        for mask in order:
            to_all(mask, share_in.at[here], share_in.at[here], 1).start()
        for copy in bias_rows:
            copy.start()
        for mask in range(1, n_rows):
            bias_rows[mask - 1].wait_recv()
            bias_sum = bias_sum + bias_in[n_rep - 2 + mask]
        bgrad_ref[...] = bias_sum
        for copy in sends + exchange + bias_rep + bias_rows:
            copy.wait_send()
        others = share_in.at[pl.ds(0, n_all - 1)]
        pltpu.make_async_copy(piece_in, piece_in, d_sem.at[0]).wait()
        pltpu.make_async_copy(others, others, d_sem.at[3]).wait()
        for index in range(n_all):
            wgrad_ref[place_of(index)] = share_in[index].astype(jnp.float32)
        pltpu.make_async_copy(others, others, d_sem.at[2]).wait()
        return

    for place in range(n_rep):
        term[place, :own_rows] = weight_term[place * own_rows:(place + 1) * own_rows]
        term[place, own_rows:] = bias_term
    scatter = [
        to_rep(mask, term.at[xor(rep, mask)], term_in.at[mask - 1], w1_send.at[mask - 1], w1_recv.at[mask - 1])
        for mask in range(1, n_rep)
    ]
    for copy in reversed(scatter):
        copy.start()
    out_ref[...] = (preact * sigma).astype(jnp.bfloat16)
    mine = term[rep]
    for mask in range(1, n_rep):
        scatter[mask - 1].wait_recv()
        mine = mine + term_in[mask - 1]
    base = pl.multiple_of(rep * own_rows, own_rows)
    pending = []
    step = 0
    while (1 << step) < n_rows:
        ring[step] = mine
        copy = to_rows(1 << step, ring.at[step], ring_in.at[step], w2_send.at[step], w2_recv.at[step])
        copy.start()
        copy.wait_recv()
        mine = mine + ring_in[step]
        pending.append(copy)
        step += 1
    wgrad_ref[pl.ds(base, own_rows)] = mine[:own_rows]

    def slab_of(index):
        return wgrad_ref.at[pl.ds(pl.multiple_of(index * own_rows, own_rows), own_rows)]

    final = [
        to_rep(mask, slab_of(rep), slab_of(rep), w4_send.at[mask - 1], w4_recv.at[mask - 1])
        for mask in range(1, n_rep)
    ]
    for copy in reversed(final):
        copy.start()
    bgrad_ref[...] = jnp.sum(mine[own_rows:], axis=0, keepdims=True)
    for copy in sends + exchange + scatter + pending + final:
        copy.wait_send()
    for mask in range(1, n_rep):
        where = slab_of(xor(rep, mask))
        to_rep(mask, where, where, w4_send.at[mask - 1], w4_recv.at[mask - 1]).wait_recv()


def shards(features, weight, bias_terms, tile_data, tile_row, tile_col, tile_count, grad_out):
    n_rows, n_rep = lax.axis_size("rows"), lax.axis_size("rep")
    block, width = features.shape
    capacity = tile_data.shape[2]
    own_rows = width // n_rep
    n_all = n_rows * n_rep
    direct = width * width == n_all * 16 * 128
    steps = 1 if direct else (n_rows - 1).bit_length()
    places = n_all if direct else 2
    whole = (own_rows + 8, width)
    vmem = pl.BlockSpec(memory_space=pltpu.VMEM)
    hbm = pl.BlockSpec(memory_space=pl.ANY)
    dma = pltpu.SemaphoreType.DMA
    layer_out, weight_grad, bias_grad = pl.pallas_call(
        functools.partial(kernel, n_rows, n_rep, direct),
        out_shape=(
            jax.ShapeDtypeStruct((block, width), jnp.bfloat16),
            jax.ShapeDtypeStruct((width, width), jnp.float32),
            jax.ShapeDtypeStruct((1, width), jnp.float32),
        ),
        in_specs=[hbm] * 8,
        out_specs=(vmem, vmem, vmem),
        scratch_shapes=[
            pltpu.VMEM((n_rows, block, width), jnp.bfloat16),
            pltpu.VMEM((capacity, block, block), jnp.bfloat16),
            pltpu.VMEM((width, width), jnp.bfloat16),
            pltpu.VMEM((1, width), jnp.float32),
            pltpu.VMEM((block, width), jnp.bfloat16),
            pltpu.VMEM((n_rep - 1, block, width), jnp.bfloat16),
            pltpu.VMEM((n_rep - 1, block, width), jnp.bfloat16),
            pltpu.VMEM((n_rep,) + whole, jnp.float32),
            pltpu.VMEM((n_rep - 1,) + whole, jnp.float32),
            pltpu.VMEM((steps,) + whole, jnp.float32),
            pltpu.VMEM((steps,) + whole, jnp.float32),
            pltpu.VMEM((2, 1, width), jnp.float32),
            pltpu.VMEM((n_rep + n_rows - 2, 1, width), jnp.float32),
            pltpu.VMEM((places, 16, 128), jnp.bfloat16),
            pltpu.VMEM((places - 1, 16, 128), jnp.bfloat16),
            pltpu.VMEM((places, 16, 128), SHARE_TYPE),
            pltpu.SMEM(tile_row.shape, jnp.int32),
            pltpu.SMEM(tile_col.shape, jnp.int32),
            pltpu.SMEM(tile_count.shape, jnp.int32),
            dma((8,)),
            dma((n_rows,)), dma((n_rows,)),
            dma((n_rep - 1,)), dma((n_rep - 1,)),
            dma((n_rep - 1,)), dma((n_rep - 1,)),
            dma((steps,)), dma((steps,)),
            dma((n_rep - 1,)), dma((n_rep - 1,)),
            dma((4,)),
            dma((2, n_rep + n_rows - 2)),
        ],
        compiler_params=pltpu.CompilerParams(
            collective_id=0, has_side_effects=True, vmem_limit_bytes=62 * 1024 * 1024),
    )(features, weight, bias_terms.reshape(1, width), tile_data, tile_row, tile_col, tile_count, grad_out)
    return layer_out, weight_grad, bias_grad.reshape(width)


def solution(mesh):
    placed = (
        P(("rows", "rep"), None),
        P(),
        P(),
        P("rows", None, None, None, None),
        P("rows", None, None),
        P("rows", None, None),
        P("rows", None),
        P(("rows", "rep"), None),
    )
    return jax.shard_map(
        shards,
        mesh=mesh,
        in_specs=placed,
        out_specs=(P(("rows", "rep"), None), P(), P()),
        check_vma=False,
    )
```

time: 48.5 us -> 37.5 us (0.77)
  Pallas kernels: 39.8 us -> 33 us
  local copies, waits for them, and re-layouts: 7.74 us -> 3.71 us
    pallas_call x1, Pallas kernels: 39.8 us -> 33 us  [shards(): pl.pallas_call(functools.partial(kernel, n_rows, n_rep, direct), out_shap...]
    unnamed x19 -> x5, local copies, waits for them, and re-layouts: 7.74 us -> 3.71 us
where the time goes in v2:
time: 37.5 us; the launch traced here: 37.4 us
  Pallas kernels  33 us (88%)
  local copies, waits for them, and re-layouts  3.71 us (10%)
  between operations  0.64 us (2%)
    pallas_call x1, Pallas kernels, shards(): pl.pallas_call(functools.partial(kernel, n_rows, n_rep, direct), out_shap...  33 us
    unnamed x5, local copies, waits for them, and re-layouts  3.71 us

profile of v2, /device:TPU:0, one launch (start us, length us, event | category | flops | bytes accessed | tf_op | source)
XLA Modules:
  0.0 37.4 jit_solution(7394774505361114609)
XLA Ops:
  0.6 33.0 %shard_map.103 = (bf16[128,256]{1,0:T(8,128)(2,1)}, f32[256,256]{1,0:T(8,128)}, f32[1,256]{1,0:T(1,128)}) custom-call(bf16[128,256]{1,0:T(8,128)(2,1)} %feat_hbm.1, bf16[256,256]{1,0:T(8,128)(2,1)} %weight_hbm.1, f32[1,256]{1,0:T(1,128)} %bitcast.3, bf16[1,4,8,128,128]{4,3,2,1,0:T(8,128)(2,1)} %tile_hbm.1, s32[1,4,8]{2,1,0:T(4,128)} %row_hbm.1, ...), custom_call_target="tpu_custom_call" | custom-call | tf_op jit(solution)/shard_map/pallas_call | solution.py:246
  33.6 1.5 %copy.14 = bf16[128,256]{1,0:T(8,128)(2,1)} copy(bf16[128,256]{1,0:T(8,128)(2,1)} %get-tuple-element.12) | data formatting | bytes 131072
  35.1 0.0 copy-start
  35.1 1.7 %copy.15 = f32[256,256]{1,0:T(8,128)} copy(f32[256,256]{1,0:T(8,128)} %get-tuple-element.13) | data formatting | bytes 524288
  36.8 0.0 copy-done
  36.8 0.6 %copy.16 = f32[256]{0:T(256)} copy(f32[256]{0:T(256)S(1)} %bitcast.2) | data formatting | bytes 2048
Async XLA Ops:
  35.1 1.7 %copy-start = (f32[1,256]{1,0:T(1,128)S(1)}, f32[1,256]{1,0:T(1,128)}, u32[]{:S(2)}) copy-start(f32[1,256]{1,0:T(1,128)} %get-tuple-element.8) | copy-start | bytes 3076

commit v3 on v2

--- a/solution.py
+++ b/solution.py
@@ -8,7 +8,6 @@
 from jax.sharding import PartitionSpec as P
 
 MESH = pl.DeviceIdType.MESH
-SHARE_TYPE = jnp.bfloat16
 
 
 def xor(value, mask):
@@ -24,7 +23,8 @@
     n_rows, n_rep, direct,
     feat_hbm, weight_hbm, bias_hbm, tile_hbm, row_hbm, col_hbm, count_hbm, gout_hbm,
     out_ref, wgrad_ref, bgrad_ref,
-    feat, tiles, weight, bias, gout, part, part_in, term, term_in, ring, ring_in, bias_out, bias_in, piece, piece_in, share_in,
+    feat, tiles, weight, bias, gout, part, part_in, term, term_in, ring, ring_in, bias_out, bias_in,
+    halves, half_in, piece, piece_in, share_in,
     row_ref, col_ref, count_ref, local_sem, g_send, g_recv, x_send, x_recv, w1_send, w1_recv,
     w2_send, w2_recv, w4_send, w4_recv, d_sem, b_sem,
 ):
@@ -61,12 +61,12 @@
     ]
     for load in loads:
         load.start()
+    loads[0].wait()
     pl.semaphore_wait(barrier, n_rows + n_rep - 2)
 
     def gather(mask, block_mask, sem):
         where = feat.at[xor(me, block_mask)]
-        source = feat_hbm if block_mask == 0 else where
-        return to_rows(mask, source, where, g_send.at[sem], g_recv.at[sem])
+        return to_rows(mask, where, where, g_send.at[sem], g_recv.at[sem])
 
     sends = [gather(1, 0, 1)]
     for mask in range(2, n_rows, 2):
@@ -85,7 +85,6 @@
         sends.append(send)
     for mask in range(1, n_rows, 2):
         arrived(mask)
-    loads[0].wait()
     loads[1].wait()
     for load in loads[5:]:
         load.wait()
@@ -125,8 +124,8 @@
         propagated, grad_pre, (((0,), (0,)), ((), ())), preferred_element_type=jnp.float32)
     bias_term = jnp.sum(grad_pre.astype(jnp.float32).reshape(block // 8, 8, width), axis=0)
     if direct:
-        n_all = n_rows * n_rep
-        here = me * n_rep + rep
+        n_pairs = n_rows * n_rep // 2
+        pair, side = me * (n_rep // 2) + rep // 2, rep % 2
         piece_rows, piece_cols = piece.shape[1:]
         across = width // piece_cols
 
@@ -134,17 +133,16 @@
             top, left = index // across * piece_rows, index % across * piece_cols
             return slice(top, top + piece_rows), slice(left, left + piece_cols)
 
-        def to_all(mask, src, dst, stage):
-            peer = (xor(me, mask // n_rep), xor(rep, mask % n_rep))
+        def to_pair(mask, src, dst, stage):
+            peer = (xor(me, mask // (n_rep // 2)), xor(rep, mask % (n_rep // 2) * 2))
             return pltpu.make_async_remote_copy(
                 src_ref=src, dst_ref=dst, send_sem=d_sem.at[2 * stage], recv_sem=d_sem.at[2 * stage + 1],
                 device_id=peer, device_id_type=MESH)
 
-        order = sorted(range(1, n_all), key=lambda mask: -mask)
-        for index in range(n_all):
-            piece[index] = weight_term[place_of(index)].astype(jnp.bfloat16)
-        for mask in order:
-            to_all(mask, piece.at[xor(here, mask)], piece_in.at[mask - 1], 0).start()
+        for index in range(2 * n_pairs):
+            halves[index % 2, index // 2] = weight_term[place_of(index)]
+        fold = to_rep(1, halves.at[xor(side, 1)], half_in, d_sem.at[4], d_sem.at[5])
+        fold.start()
         bias_out[0] = jnp.sum(bias_term, axis=0, keepdims=True)
         bias_rep = [
             to_rep(mask, bias_out.at[0], bias_in.at[mask - 1], b_sem.at[0, mask - 1], b_sem.at[1, mask - 1])
@@ -153,6 +151,11 @@
         for copy in bias_rep:
             copy.start()
         out_ref[...] = (preact * sigma).astype(jnp.bfloat16)
+        order = list(range(n_pairs - 1, 0, -1))
+        fold.wait_recv()
+        piece[...] = (halves[side] + half_in[...]).astype(jnp.bfloat16)
+        for mask in order:
+            to_pair(mask, piece.at[xor(pair, mask)], piece_in.at[mask - 1], 0).start()
         bias_sum = bias_out[0]
         for mask in range(1, n_rep):
             bias_rep[mask - 1].wait_recv()
@@ -163,27 +166,31 @@
                     b_sem.at[0, n_rep - 2 + mask], b_sem.at[1, n_rep - 2 + mask])
             for mask in range(1, n_rows)
         ]
-        done = piece[here].astype(jnp.float32)
-        pltpu.make_async_copy(piece_in, piece_in, d_sem.at[1]).wait()
-        for mask in range(1, n_all):
-            done = done + piece_in[mask - 1].astype(jnp.float32)
-        share_in[here] = done.astype(share_in.dtype)
-        for mask in order:
-            to_all(mask, share_in.at[here], share_in.at[here], 1).start()
         for copy in bias_rows:
             copy.start()
+        done = piece[pair].astype(jnp.float32)
+        pltpu.make_async_copy(piece_in, piece_in, d_sem.at[1]).wait()
+        for mask in range(1, n_pairs):
+            done = done + piece_in[mask - 1].astype(jnp.float32)
+        share_in[side, pair] = done.astype(jnp.bfloat16)
+        for mask in order:
+            to_pair(mask, share_in.at[side, pair], share_in.at[side, pair], 1).start()
         for mask in range(1, n_rows):
             bias_rows[mask - 1].wait_recv()
             bias_sum = bias_sum + bias_in[n_rep - 2 + mask]
         bgrad_ref[...] = bias_sum
-        for copy in sends + exchange + bias_rep + bias_rows:
+        for copy in sends + exchange + bias_rep + bias_rows + [fold]:
             copy.wait_send()
-        others = share_in.at[pl.ds(0, n_all - 1)]
         pltpu.make_async_copy(piece_in, piece_in, d_sem.at[0]).wait()
-        pltpu.make_async_copy(others, others, d_sem.at[3]).wait()
-        for index in range(n_all):
-            wgrad_ref[place_of(index)] = share_in[index].astype(jnp.float32)
-        pltpu.make_async_copy(others, others, d_sem.at[2]).wait()
+        pltpu.make_async_copy(piece_in, piece_in, d_sem.at[3]).wait()
+        hand = to_rep(1, share_in.at[side], share_in.at[side], d_sem.at[6], d_sem.at[7])
+        hand.start()
+        theirs = share_in.at[xor(side, 1)]
+        to_rep(1, theirs, theirs, d_sem.at[6], d_sem.at[7]).wait_recv()
+        for index in range(2 * n_pairs):
+            wgrad_ref[place_of(index)] = share_in[index % 2, index // 2].astype(jnp.float32)
+        hand.wait_send()
+        pltpu.make_async_copy(piece_in, piece_in, d_sem.at[2]).wait()
         return
 
     for place in range(n_rep):
@@ -230,6 +237,12 @@
         to_rep(mask, where, where, w4_send.at[mask - 1], w4_recv.at[mask - 1]).wait_recv()
 
 
+def deliver(first, second, third, first_out, second_out, third_out):
+    first_out[...] = first[...]
+    second_out[...] = second[...]
+    third_out[...] = third[...]
+
+
 def shards(features, weight, bias_terms, tile_data, tile_row, tile_col, tile_count, grad_out):
     n_rows, n_rep = lax.axis_size("rows"), lax.axis_size("rep")
     block, width = features.shape
@@ -238,7 +251,7 @@
     n_all = n_rows * n_rep
     direct = width * width == n_all * 16 * 128
     steps = 1 if direct else (n_rows - 1).bit_length()
-    places = n_all if direct else 2
+    pairs = n_all // 2 if direct else 2
     whole = (own_rows + 8, width)
     vmem = pl.BlockSpec(memory_space=pltpu.VMEM)
     hbm = pl.BlockSpec(memory_space=pl.ANY)
@@ -266,9 +279,11 @@
             pltpu.VMEM((steps,) + whole, jnp.float32),
             pltpu.VMEM((2, 1, width), jnp.float32),
             pltpu.VMEM((n_rep + n_rows - 2, 1, width), jnp.float32),
-            pltpu.VMEM((places, 16, 128), jnp.bfloat16),
-            pltpu.VMEM((places - 1, 16, 128), jnp.bfloat16),
-            pltpu.VMEM((places, 16, 128), SHARE_TYPE),
+            pltpu.VMEM((2, pairs, 16, 128), jnp.float32),
+            pltpu.VMEM((pairs, 16, 128), jnp.float32),
+            pltpu.VMEM((pairs, 16, 128), jnp.bfloat16),
+            pltpu.VMEM((pairs - 1, 16, 128), jnp.bfloat16),
+            pltpu.VMEM((2, pairs, 16, 128), jnp.bfloat16),
             pltpu.SMEM(tile_row.shape, jnp.int32),
             pltpu.SMEM(tile_col.shape, jnp.int32),
             pltpu.SMEM(tile_count.shape, jnp.int32),
@@ -278,12 +293,18 @@
             dma((n_rep - 1,)), dma((n_rep - 1,)),
             dma((steps,)), dma((steps,)),
             dma((n_rep - 1,)), dma((n_rep - 1,)),
-            dma((4,)),
+            dma((8,)),
             dma((2, n_rep + n_rows - 2)),
         ],
         compiler_params=pltpu.CompilerParams(
             collective_id=0, has_side_effects=True, vmem_limit_bytes=62 * 1024 * 1024),
     )(features, weight, bias_terms.reshape(1, width), tile_data, tile_row, tile_col, tile_count, grad_out)
+    layer_out, weight_grad, bias_grad = pl.pallas_call(
+        deliver,
+        out_shape=tuple(jax.ShapeDtypeStruct(x.shape, x.dtype) for x in (layer_out, weight_grad, bias_grad)),
+        in_specs=[vmem] * 3,
+        out_specs=(vmem,) * 3,
+    )(layer_out, weight_grad, bias_grad)
     return layer_out, weight_grad, bias_grad.reshape(width)
 
 

time: 37.5 us -> 34.8 us (0.928)
  local copies, waits for them, and re-layouts: 3.71 us -> 0 us
  Pallas kernels: 33 us -> 34 us
    unnamed x5 -> x0, local copies, waits for them, and re-layouts: 3.71 us -> none
    pallas_call x0 -> x1, Pallas kernels: none -> 1.69 us  [shards(): pl.pallas_call(deliver, out_shape=tuple((jax.ShapeDtypeStruct(x.shape, x....]
    pallas_call x1, Pallas kernels: 33 us -> 32.3 us  [shards(): pl.pallas_call(functools.partial(kernel, n_rows, n_rep, direct), out_shap...]
where the time goes in v3:
time: 34.8 us; the launch traced here: 34.6 us
  Pallas kernels  34 us (98%)
  between operations  0.64 us (2%)
    pallas_call x1, Pallas kernels, shards(): pl.pallas_call(functools.partial(kernel, n_rows, n_rep, direct), out_shap...  32.3 us
    pallas_call x1, Pallas kernels, shards(): pl.pallas_call(deliver, out_shape=tuple((jax.ShapeDtypeStruct(x.shape, x....  1.69 us

profile of v3, /device:TPU:0, one launch (start us, length us, event | category | flops | bytes accessed | tf_op | source)
XLA Modules:
  0.0 34.6 jit_solution(5484868337906480113)
XLA Ops:
  0.6 32.3 %shard_map.103 = (bf16[128,256]{1,0:T(8,128)(2,1)}, f32[256,256]{1,0:T(8,128)}, f32[1,256]{1,0:T(1,128)}) custom-call(bf16[128,256]{1,0:T(8,128)(2,1)} %feat_hbm.1, bf16[256,256]{1,0:T(8,128)(2,1)} %weight_hbm.1, f32[1,256]{1,0:T(1,128)} %bitcast.2, bf16[1,4,8,128,128]{4,3,2,1,0:T(8,128)(2,1)} %tile_hbm.1, s32[1,4,8]{2,1,0:T(4,128)} %row_hbm.1, ...), custom_call_target="tpu_custom_call" | custom-call | tf_op jit(solution)/shard_map/pallas_call | solution.py:259
  32.9 1.7 %shard_map.104 = (bf16[128,256]{1,0:T(8,128)(2,1)}, f32[256,256]{1,0:T(8,128)}, f32[1,256]{1,0:T(1,128)}) custom-call(bf16[128,256]{1,0:T(8,128)(2,1)} %get-tuple-element.9.first, f32[256,256]{1,0:T(8,128)} %get-tuple-element.10.second, f32[1,256]{1,0:T(1,128)} %get-tuple-element.11.third), custom_call_target="tpu_custom_call" | custom-call | tf_op jit(solution)/shard_map/pallas_call | solution.py:302
